TPU v7x, 512 devices: a whole 4x8x8 slice. The times are simulated.
512 devices in a mesh: dp: 4 (over x), ctx: 16 (over y, core), head: 8 (over z).
Axes of the slice: x: 4, y: 8, z: 8, core: 2. Of those that a mesh axis runs over, the one named last changes fastest.
Arguments:
- queries: bfloat16 [16384, 8192], P(('dp', 'ctx'), 'head'), parts along dimension 0, may hold values from -128 to 128, as said below
- keys: bfloat16 [16384, 1024], P(('dp', 'ctx'), 'head'), parts along dimension 0, may hold values from -6 to 6, as said below
- values: bfloat16 [16384, 1024], P(('dp', 'ctx'), 'head'), parts along dimension 0, may hold values from -6 to 6
- segment_ids: int32 [16384], P(('dp', 'ctx')), parts along dimension 0, may hold values from 0 to 2, never falling along the last dimension, each value on 1 to 3072 neighbouring positions
Outputs:
- attended: bfloat16 [16384, 8192], P(('dp', 'ctx'), 'head'), parts along dimension 0
There are 4 independent parts, one for each index of `dp`. A program takes and returns all parts, laid end to end along the dimension named above; each array names one. Nothing has to cross between parts.
Inputs may be any that keep to these rules, and one draw needn't show every extreme that they name: queries: entries stay within the range. keys: entries stay within the range.
All inputs are finite; a program needn't handle non-finite values.
Results may differ from a plain program's by a relative error of at most 0.005.
Values may be sent and summed in bfloat16 or wider, within the bound.
A program may use at most 128 MiB of HBM per device.

v0:
```python
import jax
import jax.numpy as jnp
from jax import lax
from jax.sharding import PartitionSpec as P

QH = 64
KVH = 8
HD = 128


def attend(members, keys, values, seg_wire):
    rows, groups, repeat, width = members[0][0].shape
    scale = width ** (-0.5)
    bounds = [(jnp.max(member[1]), jnp.min(member[2]), jnp.max(member[2])) for member in members]
    init = tuple(
        (
            (
                jnp.full((member[0].shape[0], groups, repeat), -1e30, jnp.float32),
                jnp.zeros((member[0].shape[0], groups, repeat), jnp.float32),
                jnp.zeros((member[0].shape[0], groups, repeat, width), jnp.float32),
            )
            for member in members
        )
    )
    start = jnp.int32(0)
    key_piece = lax.all_gather(keys, "ctx", axis=0, tiled=True)
    value_piece = lax.all_gather(values, "ctx", axis=0, tiled=True)
    seg_piece = lax.all_gather(seg_wire, "ctx", axis=0, tiled=True)
    count = key_piece.shape[0]
    key3 = key_piece.reshape(count, groups, width)
    value3 = value_piece.reshape(count, groups, width)
    key_pos = jnp.arange(count, dtype=jnp.int32)
    updated = []
    for fold_member, state_in, limits in zip(members, init, bounds):
        query4, query_pos, query_seg = fold_member
        last_pos, low_seg, high_seg = limits

        def update(state, query4=query4, query_pos=query_pos, query_seg=query_seg):
            running, summed, accum = state
            score = (
                jnp.einsum("rkpd,nkd->rkpn", query4, key3, preferred_element_type=jnp.float32)
                * scale
            )
            visible = (key_pos[None, :] <= query_pos[:, None]) & (
                seg_piece[None, :] == query_seg[:, None]
            )
            visible = visible[:, None, None, :]
            score = jnp.where(visible, score, -1e30)
            fresh = jnp.maximum(running, jnp.max(score, axis=-1))
            weight = jnp.where(visible, jnp.exp(score - fresh[..., None]), 0.0)
            summed = jnp.sum(weight, axis=-1)
            contrib = jnp.einsum(
                "rkpn,nkd->rkpd",
                weight.astype(jnp.bfloat16),
                value3,
                preferred_element_type=jnp.float32,
            )
            accum = contrib
            return (fresh, summed, accum)

        live = (start <= last_pos) & (seg_piece[0] <= high_seg) & (seg_piece[count - 1] >= low_seg)
        updated.append(lax.cond(live, update, lambda state: state, state_in))
    finals = tuple(updated)
    outputs = []
    for member, final in zip(members, finals):
        running, summed, accum = final
        output = accum / summed[..., None]
        outputs.append(
            output.reshape(member[0].shape[0], groups * repeat * width).astype(jnp.bfloat16)
        )
    return outputs


def per_device(queries, keys, values, segment_ids):
    rows = queries.shape[0]
    groups = keys.shape[1] // HD
    repeat = QH // KVH
    seg_wire = segment_ids.astype(jnp.bfloat16)
    place = lax.axis_index("ctx")
    query4 = queries.reshape(rows, groups, repeat, HD)
    query_pos = place * rows + jnp.arange(rows, dtype=jnp.int32)
    return attend([(query4, query_pos, seg_wire)], keys, values, seg_wire)[0]


def solution(mesh):
    in_specs = (
        P(("dp", "ctx"), "head"),
        P(("dp", "ctx"), "head"),
        P(("dp", "ctx"), "head"),
        P(("dp", "ctx")),
    )
    out_specs = P(("dp", "ctx"), "head")
    return jax.shard_map(
        per_device, mesh=mesh, in_specs=in_specs, out_specs=out_specs, check_vma=False
    )
```

profile of v0, /device:TPU:57, one launch (start us, length us, event | category | flops | bytes accessed | tf_op | source)
XLA Modules:
  0.0 151.2 jit_solution(4675875045205574048)
XLA Ops:
  6.5 0.0 all-gather.4.cloned.1.call-start
  6.5 0.7 all-gather.4.cloned.1.call-update
  7.3 0.0 all-gather.6.cloned.1.call-start
  7.3 0.7 all-gather.6.cloned.1.call-update
  8.0 0.6 fusion.18
  8.6 1.4 fusion.19
  10.0 18.5 %all-gather = bf16[16,1,256]{2,1,0:T(2,128)(2,1)S(1)} all-gather(bf16[1,1,256]{2,1,0:T(2,128)(2,1)S(1)} %reshape.85), channel_id=1, replica_groups=mesh['dp'=4,'ctx'=16,'head'=8] {'ctx'}, dimensions={0}, use_global_device_ids=true | all-gather | bytes 8704 | tf_op jit(solution)/shard_map/all_gather | solution.py:28
  29.3 0.6 fusion.20
  32.4 21.1 %all-gather.4.cloned.1.call-done = bf16[4096,128]{1,0:T(8,128)(2,1)} async-done(((bf16[256,128]{1,0:T(8,128)(2,1)}), bf16[4096,128]{1,0:T(8,128)(2,1)}) %all-gather.4.cloned.1.call-update) | async-done | bytes 1048592 | tf_op jit(solution)/shard_map/all_gather | solution.py:26
  53.5 42.0 %all-gather.6.cloned.1.call-done = bf16[4096,128]{1,0:T(8,128)(2,1)} async-done(((bf16[256,128]{1,0:T(8,128)(2,1)}), bf16[4096,128]{1,0:T(8,128)(2,1)}) %all-gather.6.cloned.1.call-update) | async-done | bytes 1048592 | tf_op jit(solution)/shard_map/all_gather | solution.py:27
  95.5 47.3 %conditional.1 = (f32[256,1,8]{0,2,1:T(8,128)S(1)}, f32[256,1,8,128]{3,0,2,1:T(8,128)S(1)}) conditional(s32[]{:T(128)} %convert_element_type.16, () %tuple.13, (s32[4096]{0:T(1024)S(1)}, s32[256]{0:T(256)S(1)}, bf16[4096]{0:T(1024)(128)(2,1)S(1)}, bf16[256]{0:T(256)(128)(2,1)S(1)}, bf16[256,1024]{1,0:T(8,128)(2,1)}, ...), branch_computations={%region_3.0_spmd, %region_4.7_spmd} | conditional | flops 4409260032 | bytes 112797224 | solution.py:62
  95.5 0.0 copy-start
  95.5 2.9 %compare_and_fusion = pred[256,4096]{0,1:T(8,128)(4,1)S(1)} fusion(s32[256]{0:T(256)S(1)} %get-tuple-element.23, s32[4096]{0:T(1024)S(1)} %get-tuple-element.22, bf16[256]{0:T(256)(128)(2,1)S(1)} %get-tuple-element.25, bf16[4096]{0:T(1024)(128)(2,1)S(1)} %get-tuple-element.24), kind=kLoop, calls=%fused_computation.8 | loop fusion | flops 5242880 | bytes 1074688 | tf_op jit(solution)/shard_map/cond/branch_1_fun/and | solution.py:44
  98.3 14.5 %fusion = (f32[256,8]{0,1:T(8,128)S(1)}, f32[4096,256,8]{1,0,2:T(8,128)}) fusion(pred[256,4096]{0,1:T(8,128)(4,1)S(1)} %compare_and_fusion, bf16[4096,128]{1,0:T(8,128)(2,1)} %get-tuple-element.26, bf16[256,1024]{1,0:T(8,128)(2,1)} %get-tuple-element.34), kind=kOutput, calls=%fused_computation.2 | convolution fusion | flops 2172647424 | bytes 36184064 | tf_op jit(solution)/shard_map/cond/branch_1_fun/rkpd,nkd->rkpn/dot_general | solution.py:41
  112.9 0.0 copy-done
  112.9 15.0 %fusion.7 = f32[256,1,8,128]{3,0,2,1:T(8,128)S(1)} fusion(f32[4096,256,8]{1,0,2:T(8,128)} %get-tuple-element.39, f32[256,8]{0,1:T(8,128)S(1)} %broadcast_maximum_fusion, pred[256,4096]{0,1:T(8,128)(4,1)S(1)} %compare_and_fusion, bf16[4096,128]{1,0:T(8,128)(2,1)S(1)} %copy-done), kind=kOutput, calls=%fused_computation.9 | convolution fusion | flops 2189426688 | bytes 36708352 | tf_op jit(solution)/shard_map/cond/branch_1_fun/rkpn,nkd->rkpd/dot_general | solution.py:52
  127.9 14.9 %fusion.2 = f32[256,8]{0,1:T(8,128)S(1)} fusion(f32[4096,256,8]{1,0,2:T(8,128)} %get-tuple-element.39, f32[256,8]{0,1:T(8,128)S(1)} %broadcast_maximum_fusion, pred[256,4096]{0,1:T(8,128)(4,1)S(1)} %compare_and_fusion), kind=kLoop, calls=%fused_computation.4 | loop fusion | flops 41940992 | bytes 34619392 | tf_op jit(solution)/shard_map/cond/branch_1_fun/reduce_sum | solution.py:51
  142.8 0.3 divide_convert_fusion
  143.2 0.3 copy.16
  143.5 0.9 copy.28
  (6 shorter events, 0.1 us)
Async XLA Ops:
  6.5 46.9 %all-gather.4.cloned.1.call-start = ((), (), s32[]{:S(2)}) async-start(), calls=%async_computation | async-start | bytes 1114112 | tf_op jit(solution)/shard_map/all_gather | solution.py:26
  7.3 88.2 %all-gather.6.cloned.1.call-start = ((), (), s32[]{:S(2)}) async-start(), calls=%async_computation.1 | async-start | bytes 1114112 | tf_op jit(solution)/shard_map/all_gather | solution.py:27
  95.5 17.4 %copy-start = (bf16[4096,128]{1,0:T(8,128)(2,1)S(1)}, bf16[4096,128]{1,0:T(8,128)(2,1)}, u32[]{:S(2)}) copy-start(bf16[4096,128]{1,0:T(8,128)(2,1)} %get-tuple-element.28) | copy-start | bytes 3145732 | tf_op jit(solution)/shard_map/cond
Sparse Core Ops, SparseCore 0:
  9.5 43.9 all-gather.3
  55.6 39.8 all-gather.5
where the time goes:
time: 154 us; the launch traced here: 151 us
  waiting for transfers between devices  64.5 us (42%)
  matrix products  29.6 us (19%)
  other arithmetic  20.1 us (13%)
  blocking collectives  18.5 us (12%)
  between operations  16.6 us (11%)
  local copies, waits for them, and re-layouts  1.84 us (1%)
    all_gather x1, waiting for transfers between devices, attend(): value_piece = lax.all_gather(values, 'ctx', axis=0, tiled=True)  42 us
    all_gather x1, waiting for transfers between devices, attend(): key_piece = lax.all_gather(keys, 'ctx', axis=0, tiled=True)  21.1 us
    all_gather x1, blocking collectives, attend(): seg_piece = lax.all_gather(seg_wire, 'ctx', axis=0, tiled=True)  18.5 us
    dot_general x1, matrix products, update(): jnp.einsum('rkpn,nkd->rkpd', weight.astype(jnp.bfloat16), value3, preferr...  15 us
    reduce_sum x1, other arithmetic, update(): summed = jnp.sum(weight, axis=-1)  14.9 us
    dot_general x1, matrix products, update(): jnp.einsum('rkpd,nkd->rkpn', query4, key3, preferred_element_type=jnp.flo...  14.5 us
  transfers between devices with their start and end apart: 2, of which 2 were waited for; matrix products, arithmetic and copies ran while one was open for 2% of the time, Pallas kernels for 0%

commit v1 on v0

v1 whole, which is shorter than its diff:
```python
import functools
import math

import jax
import jax.numpy as jnp
from jax import lax
from jax.experimental import pallas as pl
from jax.experimental.pallas import tpu as pltpu
from jax.sharding import PartitionSpec as P

HD = 128
MESH = pl.DeviceIdType.MESH
CHIPS = 8
SEG = 16
ONES = 16
HIDE = -(2.0**30)
UP, DOWN = (4, 3), (3, 4)
LAST = (2, 3)


def kernel(
    q_ref, k_ref, v_ref, seg_ref, out_ref,
    kv, qv, vv, sv, qseg, top, acc,
    in_sem, recv_sem, up_sem, down_sem, side_sem,
):
    rows = k_ref.shape[0]
    heads = q_ref.shape[1] // HD
    factor = math.log2(math.e) * HD**-0.5
    me = lax.axis_index("ctx")
    chip, core = me // 2, me % 2
    above = lax.rem(chip + 1, CHIPS) * 2 + core
    below = lax.rem(chip + CHIPS - 1, CHIPS) * 2 + core
    sibling = chip * 2 + 1 - core

    def up_comes(hop, part):
        return (chip >= hop) & (hop <= UP[part])

    def up_goes(hop, part):
        return (chip >= hop) & (hop < UP[part]) & (chip < CHIPS - 1)

    def down_comes(hop, part):
        return (lax.rem(chip + hop, CHIPS) <= LAST[part]) & (hop <= DOWN[part])

    def down_goes(hop, part):
        return (lax.rem(chip + hop, CHIPS) <= LAST[part]) & (hop < DOWN[part])

    def down_pair(hop):
        return (lax.rem(chip + hop, CHIPS) <= 2) & (chip >= 5) & (hop >= 2) & (hop <= 3)

    def down_used(hop, part):
        return down_pair(hop) | (down_comes(hop, part) & (hop == 4))

    cuts = (pl.ds(0, rows + SEG), pl.ds(rows + SEG, rows))

    def remote(block, part, send, target):
        return pltpu.make_async_remote_copy(
            src_ref=kv.at[block, cuts[part]],
            dst_ref=kv.at[block, cuts[part]],
            send_sem=send,
            recv_sem=recv_sem.at[block, part],
            device_id={"ctx": target},
            device_id_type=MESH,
        )

    def up_copy(hop, part):
        return remote((chip - hop) * 2 + core, part, up_sem.at[hop, part], above)

    def down_copy(hop, part):
        return remote(lax.rem(chip + hop, CHIPS) * 2 + core, part, down_sem.at[hop, part], below)

    def side_copy(source, part):
        return remote(source * 2 + core, part, side_sem.at[source, part], sibling)

    def arrived(block, part):
        remote(block, part, side_sem.at[0, part], sibling).wait_recv()

    barrier = pltpu.get_barrier_semaphore()

    def greet(target):
        pl.semaphore_signal(barrier, inc=1, device_id={"ctx": target}, device_id_type=MESH)

    from_below, to_above = chip >= 1, chip < CHIPS - 1
    from_above, to_below = chip != 3, chip != 4

    @pl.when(from_below)
    def _():
        greet(below)

    @pl.when(from_above)
    def _():
        greet(above)

    greet(sibling)

    k_in = pltpu.make_async_copy(k_ref, kv.at[me, pl.ds(0, rows)], in_sem.at[0])
    v_in = pltpu.make_async_copy(v_ref, vv, in_sem.at[1])
    q_in = pltpu.make_async_copy(q_ref, qv, in_sem.at[2])
    seg_in = pltpu.make_async_copy(seg_ref, sv, in_sem.at[3])
    seg_in.start()
    k_in.start()
    v_in.start()
    q_in.start()

    seg_in.wait()
    seg = sv[...]
    count = [
        jnp.sum(jnp.sum(jnp.where(seg <= d, 1.0, 0.0), axis=1, keepdims=True), axis=0, keepdims=True)
        for d in (0, 1)
    ]
    lane = lax.broadcasted_iota(jnp.int32, (8, HD), 1)
    low = jnp.where(lane == 1, count[0], jnp.where(lane == 2, count[1], 0.0))
    high = jnp.where(lane == 0, count[0], jnp.where(lane == 1, count[1], float(rows)))
    kv[me, rows : rows + SEG, :] = jnp.concatenate([low, high], axis=0).astype(jnp.bfloat16)

    def inside(low, high):
        place = lax.broadcasted_iota(jnp.int32, (rows, HD), 0).astype(jnp.float32)
        return (place >= low) & (place < high)

    lanes = lax.broadcasted_iota(jnp.int32, (rows, HD), 1)
    qseg[...] = jnp.where(inside(low[0:1], high[0:1]) & (lanes < 3), 1.0, 0.0).astype(jnp.bfloat16)

    def send_own(part):
        @pl.when(to_above)
        def _():
            up_copy(0, part).start()

        @pl.when(down_goes(0, part))
        def _():
            down_copy(0, part).start()

        @pl.when(core == 0)
        def _():
            side_copy(chip, part).start()

    k_in.wait()
    pl.semaphore_wait(barrier, to_above.astype(jnp.int32) + to_below.astype(jnp.int32) + 1)
    send_own(0)
    v_in.wait()
    turned = vv[...].astype(jnp.float32).T.astype(jnp.bfloat16)
    for half in range(rows // HD):
        at = rows + SEG + half * HD
        kv[me, at : at + HD, :] = turned[:, half * HD : (half + 1) * HD]
    send_own(1)
    q_in.wait()

    def keys_of(block):
        bounds = kv[block, rows : rows + SEG, :].astype(jnp.float32)
        hidden = jnp.where(inside(bounds[0:1], bounds[8:9]), 0.0, HIDE).astype(jnp.bfloat16)
        return jnp.concatenate([kv[block, 0:rows, :], hidden], axis=1)

    def values_of(block):
        first = rows + SEG
        return [kv[block, first + i * HD : first + (i + 1) * HD, :] for i in range(rows // HD)]

    def scores(keys, h):
        query = jnp.concatenate([qv[:, h * HD : (h + 1) * HD], qseg[...]], axis=1)
        return lax.dot_general(
            keys, query, (((1,), (1,)), ((), ())), preferred_element_type=jnp.float32
        )

    def attend(block, own=False):
        keys = keys_of(block)
        values = jnp.concatenate(values_of(block), axis=1)
        ones = jnp.ones((ONES, values.shape[1]), jnp.bfloat16)
        values = jnp.concatenate([values, ones], axis=0)

        def finish(h, weight, alpha):
            part = jnp.dot(values, weight, preferred_element_type=jnp.float32)
            acc[h] = part if own else acc[h] * alpha + part

        ahead, behind = scores(keys, 0), None
        for h in range(heads):
            score = ahead
            if h + 1 < heads:
                ahead = scores(keys, h + 1)
            if own:
                u = lax.broadcasted_iota(jnp.int32, score.shape, 0)
                t = lax.broadcasted_iota(jnp.int32, score.shape, 1)
                score = jnp.where(u <= t, score, HIDE)
            new, alpha = jnp.max(score, axis=0, keepdims=True), None
            if not own:
                old = top[h : h + 1, :]
                new = jnp.maximum(old, new)
                alpha = jnp.exp2((old - new) * factor)
            weight = jnp.exp2((score - new) * factor).astype(jnp.bfloat16)
            top[h : h + 1, :] = new
            if behind is not None:
                finish(*behind)
            behind = (h, weight, alpha)
        finish(*behind)

    attend(me, own=True)

    @pl.when(core == 1)
    def _():
        for part in range(2):
            arrived(sibling, part)
        attend(sibling)

    def one_round(hop, carry):
        above_source = lax.rem(chip + hop, CHIPS)
        for part in range(2):

            @pl.when(up_comes(hop, part))
            def _():
                arrived((chip - hop) * 2 + core, part)

                @pl.when(up_goes(hop, part))
                def _():
                    up_copy(hop, part).start()

                side_copy(chip - hop, part).start()

            @pl.when(down_comes(hop, part))
            def _():
                arrived(above_source * 2 + core, part)

                @pl.when(down_goes(hop, part))
                def _():
                    down_copy(hop, part).start()

                @pl.when(down_used(hop, part))
                def _():
                    side_copy(above_source, part).start()

        def one_block(i, carry):
            source = jnp.where(i < 2, chip - hop, above_source)
            other = i % 2

            @pl.when(other == 1)
            def _():
                for part in range(2):
                    arrived(source * 2 + 1 - core, part)

            attend(source * 2 + jnp.where(other == 1, 1 - core, core))
            return carry

        pairs = (chip >= hop).astype(jnp.int32) + down_pair(hop).astype(jnp.int32)
        return lax.fori_loop(0, 2 * pairs, one_block, carry)

    lax.fori_loop(1, 5, one_round, 0)

    for h in range(heads):
        share = acc[h, 0:HD, :] * (1.0 / acc[h, HD : HD + 1, :])
        out_ref[:, h * HD : (h + 1) * HD] = share.astype(jnp.bfloat16).T

    for part in range(2):

        @pl.when(core == 0)
        def _():
            side_copy(chip, part).wait_send()

        for hop in range(5):

            @pl.when(up_goes(hop, part))
            def _():
                up_copy(hop, part).wait_send()

            @pl.when(down_goes(hop, part))
            def _():
                down_copy(hop, part).wait_send()

        for hop in range(1, 5):

            @pl.when(up_comes(hop, part))
            def _():
                side_copy(chip - hop, part).wait_send()

            @pl.when(down_used(hop, part))
            def _():
                side_copy(lax.rem(chip + hop, CHIPS), part).wait_send()


def per_device(queries, keys, values, segment_ids):
    rows, width = queries.shape
    heads = width // HD
    size = 2 * rows + SEG
    operands = (queries, keys, values, segment_ids.reshape(rows // HD, HD))
    operands = [pltpu.with_memory_space_constraint(operand, pltpu.HBM) for operand in operands]
    return pl.pallas_call(
        kernel,
        out_shape=pltpu.VMEM((rows, width), jnp.bfloat16),
        in_specs=[pl.BlockSpec(memory_space=pltpu.HBM)] * 4,
        out_specs=pl.BlockSpec(memory_space=pltpu.VMEM),
        scratch_shapes=[
            pltpu.VMEM((2 * CHIPS, size, HD), jnp.bfloat16),
            pltpu.VMEM((rows, width), jnp.bfloat16),
            pltpu.VMEM((rows, HD), jnp.bfloat16),
            pltpu.VMEM((rows // HD, HD), jnp.int32),
            pltpu.VMEM((rows, HD), jnp.bfloat16),
            pltpu.VMEM((heads, rows), jnp.float32),
            pltpu.VMEM((heads, HD + ONES, rows), jnp.float32),
            pltpu.SemaphoreType.DMA((4,)),
            pltpu.SemaphoreType.DMA((2 * CHIPS, 2)),
            pltpu.SemaphoreType.DMA((4, 2)),
            pltpu.SemaphoreType.DMA((4, 2)),
            pltpu.SemaphoreType.DMA((CHIPS, 2)),
        ],
        compiler_params=pltpu.CompilerParams(
            collective_id=0, has_side_effects=True, vmem_limit_bytes=32 * 1024 * 1024
        ),
        cost_estimate=pl.CostEstimate(
            flops=4 * rows * rows * 13 * width,
            bytes_accessed=4 * rows * width,
            transcendentals=13 * rows * rows * heads,
        ),
        name="ring_attention",
    )(*operands)


def solution(mesh):
    in_specs = (
        P(("dp", "ctx"), "head"),
        P(("dp", "ctx"), "head"),
        P(("dp", "ctx"), "head"),
        P(("dp", "ctx")),
    )
    out_specs = P(("dp", "ctx"), "head")
    return jax.shard_map(
        per_device, mesh=mesh, in_specs=in_specs, out_specs=out_specs, check_vma=False
    )
```

time: 154 us -> 27.1 us (0.18); the launches traced: 151 us -> 26.9 us
  waiting for transfers between devices: 64.5 us -> 0 us
  matrix products: 29.6 us -> 0 us
  Pallas kernels: 0 us -> 26.1 us
  other arithmetic: 20.1 us -> 0 us
  blocking collectives: 18.5 us -> 0 us
  between operations: 16.6 us -> 0.01 us
    all_gather x2 -> x0, waiting for transfers between devices: 63.1 us -> none  [the longest x1 42 us: attend(): value_piece = lax.all_gather(values, 'ctx', axis=0, tiled=True)]
    dot_general x2 -> x0, matrix products: 29.6 us -> none  [the longest x1 15 us: update(): jnp.einsum('rkpn,nkd->rkpd', weight.astype(jnp.bfloat16), value3, preferr...]
    pallas_call x0 -> x1, Pallas kernels: none -> 26.1 us  [per_device(): pl.pallas_call(kernel, out_shape=pltpu.VMEM((rows, width), jnp.bfloat16),...]
    all_gather x1 -> x0, blocking collectives: 18.5 us -> none  [attend(): seg_piece = lax.all_gather(seg_wire, 'ctx', axis=0, tiled=True)]
    reduce_sum x1 -> x0, other arithmetic: 14.9 us -> none  [update(): summed = jnp.sum(weight, axis=-1)]
    and x1 -> x0, other arithmetic: 2.86 us -> none  [update(): (key_pos[None, :] <= query_pos[:, None]) & (seg_piece[None, :] == query_s...]
  transfers between devices with their start and end apart: 2 -> 0, of which waited for: 2 -> 0; matrix products, arithmetic and copies ran while one was open for 2% -> 0% of each run, Pallas kernels for 0% -> 0%
where the time goes in v1:
time: 27.1 us; the launch traced here: 26.9 us
  Pallas kernels  26.1 us (96%)
  local copies, waits for them, and re-layouts  0.8 us (3%)
    pallas_call x1, Pallas kernels, per_device(): pl.pallas_call(kernel, out_shape=pltpu.VMEM((rows, width), jnp.bfloat16),...  26.1 us
    unnamed x1, local copies, waits for them, and re-layouts  0.8 us

profile of v1, /device:TPU:57, one launch (start us, length us, event | category | flops | bytes accessed | tf_op | source)
XLA Modules:
  0.0 26.9 jit_solution(8987529601934007861)
XLA Ops:
  0.0 26.1 %ring_attention.1 = bf16[256,1024]{1,0:T(8,128)(2,1)S(1)} custom-call(bf16[256,1024]{1,0:T(8,128)(2,1)} %q_ref.1, bf16[256,128]{1,0:T(8,128)(2,1)} %k_ref.1, bf16[256,128]{1,0:T(8,128)(2,1)} %v_ref.1, s32[2,128]{1,0:T(2,128)} %bitcast.1), custom_call_target="tpu_custom_call" | custom-call | flops 3489660928 | bytes 1048576 | tf_op jit(solution)/shard_map/ring_attention/pallas_call | solution.py:280
  26.1 0.8 %copy.6 = bf16[256,1024]{1,0:T(8,128)(2,1)} copy(bf16[256,1024]{1,0:T(8,128)(2,1)S(1)} %ring_attention.1) | data formatting | bytes 1048576

commit v2 on v1

v2 whole, which is shorter than its diff:
```python
import functools
import math

import jax
import jax.numpy as jnp
from jax import lax
from jax.experimental import pallas as pl
from jax.experimental.pallas import tpu as pltpu
from jax.sharding import PartitionSpec as P

HD = 128
MESH = pl.DeviceIdType.MESH
CHIPS = 8
SEG = 16
ONES = 16
HIDE = -(2.0**30)
AHEAD = 2
UP, DOWN = (4, 3), (3, 4)
LAST = (2, 3)


def kernel(
    q_ref, k_ref, v_ref, seg_ref, out_ref,
    kv, qv, vv, sv, qseg, top, acc,
    in_sem, recv_sem, up_sem, down_sem, side_sem,
):
    rows = k_ref.shape[0]
    heads = q_ref.shape[1] // HD
    factor = math.log2(math.e) * HD**-0.5
    me = lax.axis_index("ctx")
    chip, core = me // 2, me % 2
    sibling = chip * 2 + 1 - core
    above_chip, below_chip = lax.rem(chip + 1, CHIPS), lax.rem(chip + CHIPS - 1, CHIPS)

    def up_comes(hop, part):
        return (chip >= hop) & (hop <= UP[part])

    def up_goes(hop, part):
        return (chip >= hop) & (hop < UP[part]) & (chip < CHIPS - 1)

    def down_passes(stream):
        return jnp.where(chip == 0, core == 1, core == stream)

    def down_comes(hop, part, stream):
        here = (lax.rem(chip + hop, CHIPS) <= LAST[part]) & (hop <= DOWN[part])
        return here & down_passes(stream)

    def down_goes(hop, part, stream):
        way = jnp.where(hop == 0, core == stream, down_passes(stream))
        return (lax.rem(chip + hop, CHIPS) <= LAST[part]) & (hop < DOWN[part]) & way

    def down_pair(hop):
        return (lax.rem(chip + hop, CHIPS) <= 2) & (chip >= 5) & (hop >= 2) & (hop <= 3)

    def down_hands(hop):
        return down_pair(hop) & ((hop == 3) | (core == 1))

    cuts = (pl.ds(0, rows + SEG), pl.ds(rows + SEG, rows))

    def remote(block, cut, send, receive, target):
        return pltpu.make_async_remote_copy(
            src_ref=kv.at[block, cut],
            dst_ref=kv.at[block, cut],
            send_sem=send,
            recv_sem=receive,
            device_id={"ctx": target},
            device_id_type=MESH,
        )

    def up_copy(hop, part):
        block = (chip - hop) * 2 + core
        send, receive = up_sem.at[hop, part], recv_sem.at[block, part]
        return remote(block, cuts[part], send, receive, above_chip * 2 + core)

    def down_copy(hop, part, stream):
        block = lax.rem(chip + hop, CHIPS) * 2 + stream
        send, receive = down_sem.at[hop, part, stream], recv_sem.at[block, part]
        target = below_chip * 2 + jnp.where(chip == 1, 1, stream)
        return remote(block, cuts[part], send, receive, target)

    whole = pl.ds(0, 2 * rows + SEG)

    def side_copy(source):
        block = source * 2 + core
        return remote(block, whole, side_sem.at[source], recv_sem.at[block, 0], sibling)

    def arrived(block, part):
        remote(block, cuts[part], up_sem.at[0, part], recv_sem.at[block, part], sibling).wait_recv()

    def handed(block):
        remote(block, whole, side_sem.at[0], recv_sem.at[block, 0], sibling).wait_recv()

    barrier = pltpu.get_barrier_semaphore()

    def greet(target):
        pl.semaphore_signal(barrier, inc=1, device_id={"ctx": target}, device_id_type=MESH)

    @pl.when(chip >= 1)
    def _():
        greet(below_chip * 2 + core)

    @pl.when((chip != 0) & (chip != 3))
    def _():
        greet(above_chip * 2 + core)

    @pl.when((chip == CHIPS - 1) & (core == 0))
    def _():
        greet(1)

    @pl.when((chip == 0) & (core == 1))
    def _():
        greet(2)
        greet(3)

    @pl.when((chip >= 1) | (core == 1))
    def _():
        greet(sibling)

    partners = [chip < CHIPS - 1, chip != 4, (chip == 0) & (core == 1), (chip >= 1) | (core == 0)]

    k_in = pltpu.make_async_copy(k_ref, kv.at[me, pl.ds(0, rows)], in_sem.at[0])
    v_in = pltpu.make_async_copy(v_ref, vv, in_sem.at[1])
    q_in = pltpu.make_async_copy(q_ref, qv, in_sem.at[2])
    seg_in = pltpu.make_async_copy(seg_ref, sv, in_sem.at[3])
    seg_in.start()
    k_in.start()
    v_in.start()
    q_in.start()

    seg_in.wait()
    seg = sv[...]
    count = [
        jnp.sum(jnp.sum(jnp.where(seg <= d, 1.0, 0.0), axis=1, keepdims=True), axis=0, keepdims=True)
        for d in (0, 1)
    ]
    lane = lax.broadcasted_iota(jnp.int32, (8, HD), 1)
    low = jnp.where(lane == 1, count[0], jnp.where(lane == 2, count[1], 0.0))
    high = jnp.where(lane == 0, count[0], jnp.where(lane == 1, count[1], float(rows)))
    kv[me, rows : rows + SEG, :] = jnp.concatenate([low, high], axis=0).astype(jnp.bfloat16)

    def inside(low, high):
        place = lax.broadcasted_iota(jnp.int32, (rows, HD), 0).astype(jnp.float32)
        return (place >= low) & (place < high)

    lanes = lax.broadcasted_iota(jnp.int32, (rows, HD), 1)
    qseg[...] = jnp.where(inside(low[0:1], high[0:1]) & (lanes < 3), 1.0, 0.0).astype(jnp.bfloat16)

    def send_own(part):
        @pl.when(chip < CHIPS - 1)
        def _():
            up_copy(0, part).start()

        for stream in range(2):

            @pl.when(down_goes(0, part, stream))
            def _():
                down_copy(0, part, stream).start()

    k_in.wait()
    pl.semaphore_wait(barrier, sum(partner.astype(jnp.int32) for partner in partners))
    send_own(0)
    v_in.wait()
    turned = vv[...].astype(jnp.float32).T.astype(jnp.bfloat16)
    for half in range(rows // HD):
        at = rows + SEG + half * HD
        kv[me, at : at + HD, :] = turned[:, half * HD : (half + 1) * HD]
    send_own(1)

    @pl.when(core == 0)
    def _():
        side_copy(chip).start()

    q_in.wait()

    def keys_of(block):
        bounds = kv[block, rows : rows + SEG, :].astype(jnp.float32)
        hidden = jnp.where(inside(bounds[0:1], bounds[8:9]), 0.0, HIDE).astype(jnp.bfloat16)
        return jnp.concatenate([kv[block, 0:rows, :], hidden], axis=1)

    def values_of(block):
        first = rows + SEG
        return [kv[block, first + i * HD : first + (i + 1) * HD, :] for i in range(rows // HD)]

    def scores(keys, h):
        query = jnp.concatenate([qv[:, h * HD : (h + 1) * HD], qseg[...]], axis=1)
        return [
            lax.dot_general(
                block, query, (((1,), (1,)), ((), ())), preferred_element_type=jnp.float32
            )
            for block in keys
        ]

    def attend(blocks, own=False):
        keys = [keys_of(block) for block in blocks]
        values = jnp.concatenate([piece for block in blocks for piece in values_of(block)], axis=1)
        ones = jnp.ones((ONES, values.shape[1]), jnp.bfloat16)
        values = jnp.concatenate([values, ones], axis=0)

        def finish(h, weight, alpha):
            part = jnp.dot(values, weight, preferred_element_type=jnp.float32)[: HD + 8]
            acc[h] = part if own else acc[h] * alpha + part

        ahead, behind = [scores(keys, h) for h in range(AHEAD)], None
        for h in range(heads):
            score = ahead.pop(0)
            if h + AHEAD < heads:
                ahead.append(scores(keys, h + AHEAD))
            if own:
                u = lax.broadcasted_iota(jnp.int32, (rows, rows), 0)
                t = lax.broadcasted_iota(jnp.int32, (rows, rows), 1)
                score = [jnp.where(u <= t, score[0], HIDE)]
            new, alpha = None, None
            for piece in score:
                most = jnp.max(piece, axis=0, keepdims=True)
                new = most if new is None else jnp.maximum(new, most)
            if not own:
                old = top[h : h + 1, :]
                new = jnp.maximum(old, new)
                alpha = jnp.exp2((old - new) * factor)
            weight = [jnp.exp2((piece - new) * factor).astype(jnp.bfloat16) for piece in score]
            top[h : h + 1, :] = new
            if behind is not None:
                finish(*behind)
            behind = (h, jnp.concatenate(weight, axis=0), alpha)
        finish(*behind)

    attend([me], own=True)

    def one_round(hop, carry):
        below_source = jnp.where(chip == 0, 0, chip - hop)
        above_source = lax.rem(chip + hop, CHIPS)
        for part in range(2):

            @pl.when((hop >= 1) & up_comes(hop, part))
            def _():
                arrived(below_source * 2 + core, part)

                @pl.when(up_goes(hop, part))
                def _():
                    up_copy(hop, part).start()

                if part == 1:
                    side_copy(below_source).start()

            for stream in range(2):

                @pl.when((hop >= 1) & down_comes(hop, part, stream))
                def _():
                    arrived(above_source * 2 + stream, part)

                    @pl.when(down_goes(hop, part, stream))
                    def _():
                        down_copy(hop, part, stream).start()

            if part == 1:

                @pl.when(down_hands(hop) | ((hop == 4) & (chip >= 4)))
                def _():
                    side_copy(above_source).start()

        pair = down_pair(hop)
        short = pair & (hop == 2) & (core == 1)
        doubles = jnp.where(short, 1, 2) * pair.astype(jnp.int32)
        alone = jnp.where(pair, 0, 2 * (chip >= hop).astype(jnp.int32))
        alone = jnp.where(short, 1, jnp.where(hop == 0, core, alone))
        alone = jnp.where(chip == 0, jnp.where(hop == 4, core, 0), alone)
        second = short | (hop == 0) | (chip == 0)

        def one_double(i, carry):
            @pl.when(i == 1)
            def _():
                handed(below_source * 2 + 1 - core)
                handed(above_source * 2 + 1 - core)

            side = jnp.where(i == 1, 1 - core, core)
            attend([below_source * 2 + side, above_source * 2 + side])
            return carry

        def one_block(i, carry):
            other = (i == 1) | second

            @pl.when(other)
            def _():
                handed(below_source * 2 + 1 - core)

            attend([below_source * 2 + jnp.where(other, 1 - core, core)])
            return carry

        lax.fori_loop(0, doubles, one_double, 0)
        lax.fori_loop(0, alone, one_block, 0)
        return carry

    lax.fori_loop(0, 5, one_round, 0)

    for h in range(heads):
        share = acc[h, 0:HD, :] * (1.0 / acc[h, HD : HD + 1, :])
        out_ref[:, h * HD : (h + 1) * HD] = share.astype(jnp.bfloat16).T

    for part in range(2):
        for hop in range(5):

            @pl.when(up_goes(hop, part))
            def _():
                up_copy(hop, part).wait_send()

            for stream in range(2):

                @pl.when(down_goes(hop, part, stream))
                def _():
                    down_copy(hop, part, stream).wait_send()

    @pl.when(core == 0)
    def _():
        side_copy(chip).wait_send()

    for hop in range(1, 5):

        @pl.when(chip >= hop)
        def _():
            side_copy(chip - hop).wait_send()

        @pl.when(down_hands(hop))
        def _():
            side_copy(lax.rem(chip + hop, CHIPS)).wait_send()


def per_device(queries, keys, values, segment_ids):
    rows, width = queries.shape
    heads = width // HD
    size = 2 * rows + SEG
    operands = (queries, keys, values, segment_ids.reshape(rows // HD, HD))
    operands = [pltpu.with_memory_space_constraint(operand, pltpu.HBM) for operand in operands]
    return pl.pallas_call(
        kernel,
        out_shape=pltpu.VMEM((rows, width), jnp.bfloat16),
        in_specs=[pl.BlockSpec(memory_space=pltpu.HBM)] * 4,
        out_specs=pl.BlockSpec(memory_space=pltpu.VMEM),
        scratch_shapes=[
            pltpu.VMEM((2 * CHIPS, size, HD), jnp.bfloat16),
            pltpu.VMEM((rows, width), jnp.bfloat16),
            pltpu.VMEM((rows, HD), jnp.bfloat16),
            pltpu.VMEM((rows // HD, HD), jnp.int32),
            pltpu.VMEM((rows, HD), jnp.bfloat16),
            pltpu.VMEM((heads, rows), jnp.float32),
            pltpu.VMEM((heads, HD + 8, rows), jnp.float32),
            pltpu.SemaphoreType.DMA((4,)),
            pltpu.SemaphoreType.DMA((2 * CHIPS, 2)),
            pltpu.SemaphoreType.DMA((4, 2)),
            pltpu.SemaphoreType.DMA((4, 2, 2)),
            pltpu.SemaphoreType.DMA((CHIPS,)),
        ],
        compiler_params=pltpu.CompilerParams(
            collective_id=0, has_side_effects=True, vmem_limit_bytes=32 * 1024 * 1024
        ),
        cost_estimate=pl.CostEstimate(
            flops=4 * rows * rows * 13 * width,
            bytes_accessed=4 * rows * width,
            transcendentals=13 * rows * rows * heads,
        ),
        name="ring_attention",
    )(*operands)


def solution(mesh):
    in_specs = (
        P(("dp", "ctx"), "head"),
        P(("dp", "ctx"), "head"),
        P(("dp", "ctx"), "head"),
        P(("dp", "ctx")),
    )
    out_specs = P(("dp", "ctx"), "head")
    return jax.shard_map(
        per_device, mesh=mesh, in_specs=in_specs, out_specs=out_specs, check_vma=False
    )
```

time: 27.1 us -> 26 us (0.959)
  Pallas kernels: 26.1 us -> 25 us
    pallas_call x1, Pallas kernels: 26.1 us -> 25 us  [per_device(): pl.pallas_call(kernel, out_shape=pltpu.VMEM((rows, width), jnp.bfloat16),...]
where the time goes in v2:
time: 26 us; the launch traced here: 25.8 us
  Pallas kernels  25 us (96%)
  local copies, waits for them, and re-layouts  0.8 us (3%)
    pallas_call x1, Pallas kernels, per_device(): pl.pallas_call(kernel, out_shape=pltpu.VMEM((rows, width), jnp.bfloat16),...  25 us
    unnamed x1, local copies, waits for them, and re-layouts  0.8 us

profile of v2, /device:TPU:57, one launch (start us, length us, event | category | flops | bytes accessed | tf_op | source)
XLA Modules:
  0.0 25.8 jit_solution(14585904753952781006)
XLA Ops:
  0.0 25.0 %ring_attention.1 = bf16[256,1024]{1,0:T(8,128)(2,1)S(1)} custom-call(bf16[256,1024]{1,0:T(8,128)(2,1)} %q_ref.1, bf16[256,128]{1,0:T(8,128)(2,1)} %k_ref.1, bf16[256,128]{1,0:T(8,128)(2,1)} %v_ref.1, s32[2,128]{1,0:T(2,128)} %bitcast.1), custom_call_target="tpu_custom_call" | custom-call | flops 3489660928 | bytes 1048576 | tf_op jit(solution)/shard_map/ring_attention/pallas_call | solution.py:333
  25.1 0.8 %copy.6 = bf16[256,1024]{1,0:T(8,128)(2,1)} copy(bf16[256,1024]{1,0:T(8,128)(2,1)S(1)} %ring_attention.1) | data formatting | bytes 1048576

commit v3 on v2

--- a/solution.py
+++ b/solution.py
@@ -15,7 +15,8 @@
 ONES = 16
 HIDE = -(2.0**30)
 AHEAD = 2
-UP, DOWN = (4, 3), (3, 4)
+UP = (4, 3)
+DOWN = 4
 LAST = (2, 3)
 
 
@@ -33,62 +34,55 @@
     above_chip, below_chip = lax.rem(chip + 1, CHIPS), lax.rem(chip + CHIPS - 1, CHIPS)
 
     def up_comes(hop, part):
-        return (chip >= hop) & (hop <= UP[part])
+        return (chip >= hop) & ((hop <= 3) | ((hop <= UP[part]) & (chip == CHIPS - 1)))
 
     def up_goes(hop, part):
-        return (chip >= hop) & (hop < UP[part]) & (chip < CHIPS - 1)
+        return (chip >= hop) & (chip < CHIPS - 1) & ((hop < 3) | ((hop < UP[part]) & (chip == CHIPS - 2)))
 
     def down_passes(stream):
         return jnp.where(chip == 0, core == 1, core == stream)
 
     def down_comes(hop, part, stream):
-        here = (lax.rem(chip + hop, CHIPS) <= LAST[part]) & (hop <= DOWN[part])
-        return here & down_passes(stream)
+        here = (lax.rem(chip + hop, CHIPS) <= LAST[part]) & (hop >= 1) & (hop <= DOWN)
+        return here & ((chip < CHIPS - 1) | (hop >= 2)) & down_passes(stream)
 
     def down_goes(hop, part, stream):
-        way = jnp.where(hop == 0, core == stream, down_passes(stream))
-        return (lax.rem(chip + hop, CHIPS) <= LAST[part]) & (hop < DOWN[part]) & way
+        own = (hop == 0) & (chip <= LAST[part]) & (core == stream)
+        return own | (down_comes(hop, part, stream) & (hop < DOWN))
 
     def down_pair(hop):
         return (lax.rem(chip + hop, CHIPS) <= 2) & (chip >= 5) & (hop >= 2) & (hop <= 3)
 
-    def down_hands(hop):
-        return down_pair(hop) & ((hop == 3) | (core == 1))
+    def down_hands(hop, part, stream):
+        pair = down_pair(hop) & ((hop == 3) | (core == 1))
+        return (pair | ((hop == 4) & (chip >= 4))) & down_comes(hop, part, stream)
 
     cuts = (pl.ds(0, rows + SEG), pl.ds(rows + SEG, rows))
 
-    def remote(block, cut, send, receive, target):
+    def remote(block, part, send, target):
         return pltpu.make_async_remote_copy(
-            src_ref=kv.at[block, cut],
-            dst_ref=kv.at[block, cut],
+            src_ref=kv.at[block, cuts[part]],
+            dst_ref=kv.at[block, cuts[part]],
             send_sem=send,
-            recv_sem=receive,
+            recv_sem=recv_sem.at[block, part],
             device_id={"ctx": target},
             device_id_type=MESH,
         )
 
     def up_copy(hop, part):
-        block = (chip - hop) * 2 + core
-        send, receive = up_sem.at[hop, part], recv_sem.at[block, part]
-        return remote(block, cuts[part], send, receive, above_chip * 2 + core)
+        return remote((chip - hop) * 2 + core, part, up_sem.at[hop, part], above_chip * 2 + core)
 
     def down_copy(hop, part, stream):
         block = lax.rem(chip + hop, CHIPS) * 2 + stream
-        send, receive = down_sem.at[hop, part, stream], recv_sem.at[block, part]
         target = below_chip * 2 + jnp.where(chip == 1, 1, stream)
-        return remote(block, cuts[part], send, receive, target)
-
-    whole = pl.ds(0, 2 * rows + SEG)
-
-    def side_copy(source):
-        block = source * 2 + core
-        return remote(block, whole, side_sem.at[source], recv_sem.at[block, 0], sibling)
+        target = jnp.where((chip == 0) & (hop == 0), (CHIPS - 2) * 2 + stream, target)
+        return remote(block, part, down_sem.at[hop, part, stream], target)
+
+    def side_copy(source, part):
+        return remote(source * 2 + core, part, side_sem.at[source, part], sibling)
 
     def arrived(block, part):
-        remote(block, cuts[part], up_sem.at[0, part], recv_sem.at[block, part], sibling).wait_recv()
-
-    def handed(block):
-        remote(block, whole, side_sem.at[0], recv_sem.at[block, 0], sibling).wait_recv()
+        remote(block, part, side_sem.at[0, part], sibling).wait_recv()
 
     barrier = pltpu.get_barrier_semaphore()
 
@@ -99,11 +93,15 @@
     def _():
         greet(below_chip * 2 + core)
 
-    @pl.when((chip != 0) & (chip != 3))
+    @pl.when((chip >= 1) & (chip != 3) & (chip < CHIPS - 1))
     def _():
         greet(above_chip * 2 + core)
 
-    @pl.when((chip == CHIPS - 1) & (core == 0))
+    @pl.when(chip == CHIPS - 2)
+    def _():
+        greet(core)
+
+    @pl.when(chip == CHIPS - 1)
     def _():
         greet(1)
 
@@ -116,7 +114,8 @@
     def _():
         greet(sibling)
 
-    partners = [chip < CHIPS - 1, chip != 4, (chip == 0) & (core == 1), (chip >= 1) | (core == 0)]
+    passer = (chip == 0) & (core == 1)
+    partners = [chip < CHIPS - 1, chip != 4, passer, passer, (chip >= 1) | (core == 0)]
 
     k_in = pltpu.make_async_copy(k_ref, kv.at[me, pl.ds(0, rows)], in_sem.at[0])
     v_in = pltpu.make_async_copy(v_ref, vv, in_sem.at[1])
@@ -152,9 +151,13 @@
 
         for stream in range(2):
 
-            @pl.when(down_goes(0, part, stream))
+            @pl.when((core == stream) & (chip <= LAST[part]))
             def _():
                 down_copy(0, part, stream).start()
+
+        @pl.when(core == 0)
+        def _():
+            side_copy(chip, part).start()
 
     k_in.wait()
     pl.semaphore_wait(barrier, sum(partner.astype(jnp.int32) for partner in partners))
@@ -165,11 +168,6 @@
         at = rows + SEG + half * HD
         kv[me, at : at + HD, :] = turned[:, half * HD : (half + 1) * HD]
     send_own(1)
-
-    @pl.when(core == 0)
-    def _():
-        side_copy(chip).start()
-
     q_in.wait()
 
     def keys_of(block):
@@ -229,34 +227,42 @@
     def one_round(hop, carry):
         below_source = jnp.where(chip == 0, 0, chip - hop)
         above_source = lax.rem(chip + hop, CHIPS)
+
+        def relay_up(part):
+            @pl.when((hop >= 1) & up_comes(hop, part))
+            def _():
+                arrived(below_source * 2 + core, part)
+
+                @pl.when(up_goes(hop, part))
+                def _():
+                    up_copy(hop, part).start()
+
+                side_copy(below_source, part).start()
+
+        def relay_down(part, stream, turn):
+            @pl.when(turn & down_comes(hop, part, stream))
+            def _():
+                arrived(above_source * 2 + stream, part)
+
+                @pl.when(down_goes(hop, part, stream))
+                def _():
+                    down_copy(hop, part, stream).start()
+
+                @pl.when(down_hands(hop, part, stream))
+                def _():
+                    side_copy(above_source, part).start()
+
+        first = (chip == 1) | (chip == CHIPS - 1)
         for part in range(2):
-
-            @pl.when((hop >= 1) & up_comes(hop, part))
-            def _():
-                arrived(below_source * 2 + core, part)
-
-                @pl.when(up_goes(hop, part))
-                def _():
-                    up_copy(hop, part).start()
-
-                if part == 1:
-                    side_copy(below_source).start()
-
             for stream in range(2):
-
-                @pl.when((hop >= 1) & down_comes(hop, part, stream))
-                def _():
-                    arrived(above_source * 2 + stream, part)
-
-                    @pl.when(down_goes(hop, part, stream))
-                    def _():
-                        down_copy(hop, part, stream).start()
-
-            if part == 1:
-
-                @pl.when(down_hands(hop) | ((hop == 4) & (chip >= 4)))
-                def _():
-                    side_copy(above_source).start()
+                relay_down(part, stream, first)
+            relay_up(part)
+            for stream in range(2):
+                relay_down(part, stream, jnp.logical_not(first))
+
+        def handed(block):
+            for part in range(2):
+                arrived(block, part)
 
         pair = down_pair(hop)
         short = pair & (hop == 2) & (core == 1)
@@ -297,7 +303,12 @@
         out_ref[:, h * HD : (h + 1) * HD] = share.astype(jnp.bfloat16).T
 
     for part in range(2):
-        for hop in range(5):
+
+        @pl.when(core == 0)
+        def _():
+            side_copy(chip, part).wait_send()
+
+        for hop in range(4):
 
             @pl.when(up_goes(hop, part))
             def _():
@@ -309,19 +320,17 @@
                 def _():
                     down_copy(hop, part, stream).wait_send()
 
-    @pl.when(core == 0)
-    def _():
-        side_copy(chip).wait_send()
-
-    for hop in range(1, 5):
-
-        @pl.when(chip >= hop)
-        def _():
-            side_copy(chip - hop).wait_send()
-
-        @pl.when(down_hands(hop))
-        def _():
-            side_copy(lax.rem(chip + hop, CHIPS)).wait_send()
+        for hop in range(1, 5):
+
+            @pl.when(up_comes(hop, part))
+            def _():
+                side_copy(chip - hop, part).wait_send()
+
+            for stream in range(2):
+
+                @pl.when(down_hands(hop, part, stream))
+                def _():
+                    side_copy(lax.rem(chip + hop, CHIPS), part).wait_send()
 
 
 def per_device(queries, keys, values, segment_ids):
@@ -347,7 +356,7 @@
             pltpu.SemaphoreType.DMA((2 * CHIPS, 2)),
             pltpu.SemaphoreType.DMA((4, 2)),
             pltpu.SemaphoreType.DMA((4, 2, 2)),
-            pltpu.SemaphoreType.DMA((CHIPS,)),
+            pltpu.SemaphoreType.DMA((CHIPS, 2)),
         ],
         compiler_params=pltpu.CompilerParams(
             collective_id=0, has_side_effects=True, vmem_limit_bytes=32 * 1024 * 1024

time: 26 us -> 23.1 us (0.89)
  Pallas kernels: 25 us -> 22.1 us
    pallas_call x1, Pallas kernels: 25 us -> 22.1 us  [per_device(): pl.pallas_call(kernel, out_shape=pltpu.VMEM((rows, width), jnp.bfloat16),...]
where the time goes in v3:
time: 23.1 us; the launch traced here: 22.9 us
  Pallas kernels  22.1 us (96%)
  local copies, waits for them, and re-layouts  0.8 us (3%)
    pallas_call x1, Pallas kernels, per_device(): pl.pallas_call(kernel, out_shape=pltpu.VMEM((rows, width), jnp.bfloat16),...  22.1 us
    unnamed x1, local copies, waits for them, and re-layouts  0.8 us

profile of v3, /device:TPU:57, one launch (start us, length us, event | category | flops | bytes accessed | tf_op | source)
XLA Modules:
  0.0 22.9 jit_solution(11132126603121727105)
XLA Ops:
  0.0 22.1 %ring_attention.1 = bf16[256,1024]{1,0:T(8,128)(2,1)S(1)} custom-call(bf16[256,1024]{1,0:T(8,128)(2,1)} %q_ref.1, bf16[256,128]{1,0:T(8,128)(2,1)} %k_ref.1, bf16[256,128]{1,0:T(8,128)(2,1)} %v_ref.1, s32[2,128]{1,0:T(2,128)} %bitcast.1), custom_call_target="tpu_custom_call" | custom-call | flops 3489660928 | bytes 1048576 | tf_op jit(solution)/shard_map/ring_attention/pallas_call | solution.py:342
  22.1 0.8 %copy.6 = bf16[256,1024]{1,0:T(8,128)(2,1)} copy(bf16[256,1024]{1,0:T(8,128)(2,1)S(1)} %ring_attention.1) | data formatting | bytes 1048576

commit v4 on v3

--- a/solution.py
+++ b/solution.py
@@ -15,6 +15,44 @@
 ONES = 16
 HIDE = -(2.0**30)
 AHEAD = 2
+PLAN = (
+    ("d1K", "d1V", "d2K", "d2V", "d3V", "C0"),
+    ("C0", "d1K", "u1K", "d1V", "u1V", "a1", "d2V", "b1"),
+    ("C0", "u1K", "d1V", "u1V", "a1", "u2K", "b1", "u2V", "a2", "b2"),
+    (
+        "C0", "u1K", "u1V", "a1", "u2K", "b1", "u2V", "a2", "u3K", "b2", "u3V", "a3",
+        "b3",
+    ),
+    (
+        "C0", "u1K", "u1V", "a1", "b1", "u2K", "d4K", "u2V", "a2", "d4V", "b2", "A4",
+        "u3K", "B4", "u3V", "a3", "b3",
+    ),
+    (
+        "C0", "u1K", "d3K", "u1V", "a1", "d3V", "b1", "u2K", "A3", "u2V", "a2", "B3",
+        "b2", "u3K", "d4K", "u3V", "a3", "d4V", "A4", "b3", "B4",
+    ),
+    (
+        "C0", "d2K", "u1K", "d2V", "u1V", "a1", "A2", "u2K", "b1", "d3K", "B2", "u2V",
+        "a2", "d3V", "A3", "u3K", "b2", "d4K", "u3V", "a3", "B3", "d4V", "A4", "b3",
+        "B4",
+    ),
+    (
+        "C0", "u1K", "u1V", "a1", "d2K", "b1", "u2K", "d2V", "A2", "u2V", "a2", "d3K",
+        "B2", "u3K", "b2", "d3V", "A3", "u3V", "a3", "B3", "d4V", "b3", "u4K", "a4",
+        "b4",
+    ),
+)
+KINDS = "udabABC"
+DIGITS = 5
+
+
+def word_of(steps):
+    word = 0
+    for place, step in enumerate(steps):
+        rank = 8 * KINDS.index(step[0]) + 2 * max(int(step[1]) - 1, 0) + step.endswith("V")
+        word += (rank + 1) << (6 * place)
+    return word
+
 UP = (4, 3)
 DOWN = 4
 LAST = (2, 3)
@@ -224,79 +262,89 @@
 
     attend([me], own=True)
 
-    def one_round(hop, carry):
-        below_source = jnp.where(chip == 0, 0, chip - hop)
-        above_source = lax.rem(chip + hop, CHIPS)
-
-        def relay_up(part):
-            @pl.when((hop >= 1) & up_comes(hop, part))
-            def _():
-                arrived(below_source * 2 + core, part)
-
-                @pl.when(up_goes(hop, part))
+    def relay_up(hop, part):
+        source = chip - hop
+        arrived(source * 2 + core, part)
+
+        @pl.when(up_goes(hop, part))
+        def _():
+            up_copy(hop, part).start()
+
+        side_copy(source, part).start()
+
+    def relay_down(hop, part, stream):
+        @pl.when(down_comes(hop, part, stream))
+        def _():
+            source = lax.rem(chip + hop, CHIPS)
+            arrived(source * 2 + stream, part)
+
+            @pl.when(down_goes(hop, part, stream))
+            def _():
+                down_copy(hop, part, stream).start()
+
+            @pl.when(down_hands(hop, part, stream))
+            def _():
+                side_copy(source, part).start()
+
+    def use(kind, hop):
+        other = (kind == 4) | (kind == 6) | (kind == 7)
+        source = jnp.where(kind <= 4, chip - hop, lax.rem(chip + hop, CHIPS))
+        source = jnp.where(kind == 7, chip, source)
+        unseen = other & (core == 1) & (chip - source == 6)
+        unseen = unseen | ((kind == 7) & (core == 0))
+
+        @pl.when(jnp.logical_not(unseen))
+        def _():
+            @pl.when(other)
+            def _():
+                for part in range(2):
+                    arrived(source * 2 + 1 - core, part)
+
+            attend([source * 2 + jnp.where(other, 1 - core, core)])
+
+    def one_step(_, word):
+        rank = lax.rem(word, 64) + 7
+        kind, rest = lax.div(rank, 8), lax.rem(rank, 8)
+        hop, value = lax.div(rest, 2) + 1, lax.rem(rest, 2)
+
+        @pl.when(kind == 1)
+        def _():
+            for part in range(2):
+
+                @pl.when(value == part)
                 def _():
-                    up_copy(hop, part).start()
-
-                side_copy(below_source, part).start()
-
-        def relay_down(part, stream, turn):
-            @pl.when(turn & down_comes(hop, part, stream))
-            def _():
-                arrived(above_source * 2 + stream, part)
-
-                @pl.when(down_goes(hop, part, stream))
+                    relay_up(hop, part)
+
+        @pl.when(kind == 2)
+        def _():
+            for part in range(2):
+
+                @pl.when(value == part)
                 def _():
-                    down_copy(hop, part, stream).start()
-
-                @pl.when(down_hands(hop, part, stream))
-                def _():
-                    side_copy(above_source, part).start()
-
-        first = (chip == 1) | (chip == CHIPS - 1)
-        for part in range(2):
-            for stream in range(2):
-                relay_down(part, stream, first)
-            relay_up(part)
-            for stream in range(2):
-                relay_down(part, stream, jnp.logical_not(first))
-
-        def handed(block):
-            for part in range(2):
-                arrived(block, part)
-
-        pair = down_pair(hop)
-        short = pair & (hop == 2) & (core == 1)
-        doubles = jnp.where(short, 1, 2) * pair.astype(jnp.int32)
-        alone = jnp.where(pair, 0, 2 * (chip >= hop).astype(jnp.int32))
-        alone = jnp.where(short, 1, jnp.where(hop == 0, core, alone))
-        alone = jnp.where(chip == 0, jnp.where(hop == 4, core, 0), alone)
-        second = short | (hop == 0) | (chip == 0)
-
-        def one_double(i, carry):
-            @pl.when(i == 1)
-            def _():
-                handed(below_source * 2 + 1 - core)
-                handed(above_source * 2 + 1 - core)
-
-            side = jnp.where(i == 1, 1 - core, core)
-            attend([below_source * 2 + side, above_source * 2 + side])
-            return carry
-
-        def one_block(i, carry):
-            other = (i == 1) | second
-
-            @pl.when(other)
-            def _():
-                handed(below_source * 2 + 1 - core)
-
-            attend([below_source * 2 + jnp.where(other, 1 - core, core)])
-            return carry
-
-        lax.fori_loop(0, doubles, one_double, 0)
-        lax.fori_loop(0, alone, one_block, 0)
+                    for stream in range(2):
+                        relay_down(hop, part, stream)
+
+        @pl.when(kind >= 3)
+        def _():
+            use(kind, hop)
+
+        return lax.div(word, 64)
+
+    words = []
+    for first in range(0, max(len(steps) for steps in PLAN), DIGITS):
+        word = jnp.int32(0)
+        for place, steps in enumerate(PLAN):
+            word = jnp.where(chip == place, word_of(steps[first : first + DIGITS]), word)
+        words.append(word)
+
+    def one_word(i, carry):
+        word = words[0]
+        for place in range(1, len(words)):
+            word = jnp.where(i == place, words[place], word)
+        lax.fori_loop(0, DIGITS, one_step, word)
         return carry
 
-    lax.fori_loop(0, 5, one_round, 0)
+    lax.fori_loop(0, len(words), one_word, 0)
 
     for h in range(heads):
         share = acc[h, 0:HD, :] * (1.0 / acc[h, HD : HD + 1, :])

time: 23.1 us -> 28.2 us (1.22)
  Pallas kernels: 22.1 us -> 27 us
    pallas_call x1, Pallas kernels: 22.1 us -> 27 us  [per_device(): pl.pallas_call(kernel, out_shape=pltpu.VMEM((rows, width), jnp.bfloat16),...]
where the time goes in v4:
time: 28.2 us; the launch traced here: 27.8 us
  Pallas kernels  27 us (96%)
  local copies, waits for them, and re-layouts  0.8 us (3%)
    pallas_call x1, Pallas kernels, per_device(): pl.pallas_call(kernel, out_shape=pltpu.VMEM((rows, width), jnp.bfloat16),...  27 us
    unnamed x1, local copies, waits for them, and re-layouts  0.8 us

profile of v4, /device:TPU:57, one launch (start us, length us, event | category | flops | bytes accessed | tf_op | source)
XLA Modules:
  0.0 27.8 jit_solution(6641750995023314226)
XLA Ops:
  0.0 27.0 %ring_attention.1 = bf16[256,1024]{1,0:T(8,128)(2,1)S(1)} custom-call(bf16[256,1024]{1,0:T(8,128)(2,1)} %q_ref.1, bf16[256,128]{1,0:T(8,128)(2,1)} %k_ref.1, bf16[256,128]{1,0:T(8,128)(2,1)} %v_ref.1, s32[2,128]{1,0:T(2,128)} %bitcast.1), custom_call_target="tpu_custom_call" | custom-call | flops 3489660928 | bytes 1048576 | tf_op jit(solution)/shard_map/ring_attention/pallas_call | solution.py:390
  27.0 0.8 %copy.6 = bf16[256,1024]{1,0:T(8,128)(2,1)} copy(bf16[256,1024]{1,0:T(8,128)(2,1)S(1)} %ring_attention.1) | data formatting | bytes 1048576

commit v5 on v3

--- a/solution.py
+++ b/solution.py
@@ -224,45 +224,65 @@
 
     attend([me], own=True)
 
+    def relay_up(hop, part):
+        @pl.when(up_comes(hop, part))
+        def _():
+            arrived((chip - hop) * 2 + core, part)
+
+            @pl.when(up_goes(hop, part))
+            def _():
+                up_copy(hop, part).start()
+
+            side_copy(chip - hop, part).start()
+
+    def relay_down(hop, part):
+        source = lax.rem(chip + hop, CHIPS)
+
+        def pass_on(stream):
+            @pl.when(down_comes(hop, part, stream))
+            def _():
+                arrived(source * 2 + stream, part)
+
+                @pl.when(down_goes(hop, part, stream))
+                def _():
+                    down_copy(hop, part, stream).start()
+
+                @pl.when(down_hands(hop, part, stream))
+                def _():
+                    side_copy(source, part).start()
+
+        pass_on(jnp.where(chip == 0, 0, core))
+
+        @pl.when(chip == 0)
+        def _():
+            pass_on(1)
+
+    def handed(block):
+        for part in range(2):
+            arrived(block, part)
+
     def one_round(hop, carry):
         below_source = jnp.where(chip == 0, 0, chip - hop)
         above_source = lax.rem(chip + hop, CHIPS)
-
-        def relay_up(part):
-            @pl.when((hop >= 1) & up_comes(hop, part))
-            def _():
-                arrived(below_source * 2 + core, part)
-
-                @pl.when(up_goes(hop, part))
-                def _():
-                    up_copy(hop, part).start()
-
-                side_copy(below_source, part).start()
-
-        def relay_down(part, stream, turn):
-            @pl.when(turn & down_comes(hop, part, stream))
-            def _():
-                arrived(above_source * 2 + stream, part)
-
-                @pl.when(down_goes(hop, part, stream))
-                def _():
-                    down_copy(hop, part, stream).start()
-
-                @pl.when(down_hands(hop, part, stream))
-                def _():
-                    side_copy(above_source, part).start()
-
         first = (chip == 1) | (chip == CHIPS - 1)
-        for part in range(2):
-            for stream in range(2):
-                relay_down(part, stream, first)
-            relay_up(part)
-            for stream in range(2):
-                relay_down(part, stream, jnp.logical_not(first))
-
-        def handed(block):
+        early = (chip == CHIPS - 2) & (hop == 2)
+
+        @pl.when(hop >= 1)
+        def _():
             for part in range(2):
-                arrived(block, part)
+                done = (chip == CHIPS - 2) & (hop == 3) & (part == 0)
+
+                @pl.when(first)
+                def _():
+                    relay_down(hop, part)
+
+                @pl.when(jnp.logical_not(done))
+                def _():
+                    relay_up(hop, part)
+
+                @pl.when(jnp.logical_not(first | done))
+                def _():
+                    relay_down(hop, part)
 
         pair = down_pair(hop)
         short = pair & (hop == 2) & (core == 1)
@@ -280,6 +300,12 @@
 
             side = jnp.where(i == 1, 1 - core, core)
             attend([below_source * 2 + side, above_source * 2 + side])
+
+            @pl.when(early & (i == 0))
+            def _():
+                relay_up(hop + 1, 0)
+                relay_down(hop + 1, 0)
+
             return carry
 
         def one_block(i, carry):

time: 23.1 us -> 23.8 us (1.030)
  the two profiles are of different devices: /device:TPU:57 before, /device:TPU:49 now
where the time goes in v5:
time: 23.8 us; the launch traced here: 23.7 us
  Pallas kernels  22.9 us (96%)
  local copies, waits for them, and re-layouts  0.8 us (3%)
    pallas_call x1, Pallas kernels, per_device(): pl.pallas_call(kernel, out_shape=pltpu.VMEM((rows, width), jnp.bfloat16),...  22.9 us
    unnamed x1, local copies, waits for them, and re-layouts  0.8 us

profile of v5, /device:TPU:49, one launch (start us, length us, event | category | flops | bytes accessed | tf_op | source)
XLA Modules:
  0.0 23.7 jit_solution(11805126828597094143)
XLA Ops:
  0.0 22.9 %ring_attention.1 = bf16[256,1024]{1,0:T(8,128)(2,1)S(1)} custom-call(bf16[256,1024]{1,0:T(8,128)(2,1)} %q_ref.1, bf16[256,128]{1,0:T(8,128)(2,1)} %k_ref.1, bf16[256,128]{1,0:T(8,128)(2,1)} %v_ref.1, s32[2,128]{1,0:T(2,128)} %bitcast.1), custom_call_target="tpu_custom_call" | custom-call | flops 3489660928 | bytes 1048576 | tf_op jit(solution)/shard_map/ring_attention/pallas_call | solution.py:368
  22.9 0.8 %copy.6 = bf16[256,1024]{1,0:T(8,128)(2,1)} copy(bf16[256,1024]{1,0:T(8,128)(2,1)S(1)} %ring_attention.1) | data formatting | bytes 1048576

commit v6 on v5

--- a/solution.py
+++ b/solution.py
@@ -57,7 +57,7 @@
         pair = down_pair(hop) & ((hop == 3) | (core == 1))
         return (pair | ((hop == 4) & (chip >= 4))) & down_comes(hop, part, stream)
 
-    cuts = (pl.ds(0, rows + SEG), pl.ds(rows + SEG, rows))
+    cuts = (pl.ds(0, rows), pl.ds(rows, SEG + rows))
 
     def remote(block, part, send, target):
         return pltpu.make_async_remote_copy(
@@ -121,10 +121,27 @@
     v_in = pltpu.make_async_copy(v_ref, vv, in_sem.at[1])
     q_in = pltpu.make_async_copy(q_ref, qv, in_sem.at[2])
     seg_in = pltpu.make_async_copy(seg_ref, sv, in_sem.at[3])
+    k_in.start()
     seg_in.start()
-    k_in.start()
     v_in.start()
     q_in.start()
+
+    def send_own(part):
+        @pl.when(chip < CHIPS - 1)
+        def _():
+            up_copy(0, part).start()
+
+        @pl.when(chip <= LAST[part])
+        def _():
+            down_copy(0, part, core).start()
+
+        @pl.when(core == 0)
+        def _():
+            side_copy(chip, part).start()
+
+    k_in.wait()
+    pl.semaphore_wait(barrier, sum(partner.astype(jnp.int32) for partner in partners))
+    send_own(0)
 
     seg_in.wait()
     seg = sv[...]
@@ -136,38 +153,19 @@
     low = jnp.where(lane == 1, count[0], jnp.where(lane == 2, count[1], 0.0))
     high = jnp.where(lane == 0, count[0], jnp.where(lane == 1, count[1], float(rows)))
     kv[me, rows : rows + SEG, :] = jnp.concatenate([low, high], axis=0).astype(jnp.bfloat16)
-
-    def inside(low, high):
-        place = lax.broadcasted_iota(jnp.int32, (rows, HD), 0).astype(jnp.float32)
-        return (place >= low) & (place < high)
-
-    lanes = lax.broadcasted_iota(jnp.int32, (rows, HD), 1)
-    qseg[...] = jnp.where(inside(low[0:1], high[0:1]) & (lanes < 3), 1.0, 0.0).astype(jnp.bfloat16)
-
-    def send_own(part):
-        @pl.when(chip < CHIPS - 1)
-        def _():
-            up_copy(0, part).start()
-
-        for stream in range(2):
-
-            @pl.when((core == stream) & (chip <= LAST[part]))
-            def _():
-                down_copy(0, part, stream).start()
-
-        @pl.when(core == 0)
-        def _():
-            side_copy(chip, part).start()
-
-    k_in.wait()
-    pl.semaphore_wait(barrier, sum(partner.astype(jnp.int32) for partner in partners))
-    send_own(0)
     v_in.wait()
     turned = vv[...].astype(jnp.float32).T.astype(jnp.bfloat16)
     for half in range(rows // HD):
         at = rows + SEG + half * HD
         kv[me, at : at + HD, :] = turned[:, half * HD : (half + 1) * HD]
     send_own(1)
+
+    def inside(low, high):
+        place = lax.broadcasted_iota(jnp.int32, (rows, HD), 0).astype(jnp.float32)
+        return (place >= low) & (place < high)
+
+    lanes = lax.broadcasted_iota(jnp.int32, (rows, HD), 1)
+    qseg[...] = jnp.where(inside(low[0:1], high[0:1]) & (lanes < 3), 1.0, 0.0).astype(jnp.bfloat16)
     q_in.wait()
 
     def keys_of(block):
@@ -265,22 +263,18 @@
         below_source = jnp.where(chip == 0, 0, chip - hop)
         above_source = lax.rem(chip + hop, CHIPS)
         first = (chip == 1) | (chip == CHIPS - 1)
-        early = (chip == CHIPS - 2) & (hop == 2)
 
         @pl.when(hop >= 1)
         def _():
             for part in range(2):
-                done = (chip == CHIPS - 2) & (hop == 3) & (part == 0)
 
                 @pl.when(first)
                 def _():
                     relay_down(hop, part)
 
-                @pl.when(jnp.logical_not(done))
-                def _():
-                    relay_up(hop, part)
-
-                @pl.when(jnp.logical_not(first | done))
+                relay_up(hop, part)
+
+                @pl.when(jnp.logical_not(first))
                 def _():
                     relay_down(hop, part)
 
@@ -300,12 +294,6 @@
 
             side = jnp.where(i == 1, 1 - core, core)
             attend([below_source * 2 + side, above_source * 2 + side])
-
-            @pl.when(early & (i == 0))
-            def _():
-                relay_up(hop + 1, 0)
-                relay_down(hop + 1, 0)
-
             return carry
 
         def one_block(i, carry):
@@ -334,27 +322,39 @@
         def _():
             side_copy(chip, part).wait_send()
 
+        def sent_up(hop, carry):
+            up_copy(hop, part).wait_send()
+            return carry
+
+        def handed_over(hop, carry):
+            side_copy(chip - hop, part).wait_send()
+            return carry
+
+        most = jnp.where(chip == CHIPS - 2, UP[part] - 1, 2)
+        lax.fori_loop(0, jnp.where(chip == CHIPS - 1, 0, jnp.minimum(chip, most) + 1), sent_up, 0)
+        most = jnp.where(chip == CHIPS - 1, UP[part], 3)
+        lax.fori_loop(1, jnp.minimum(chip, most) + 1, handed_over, 0)
+
         for hop in range(4):
-
-            @pl.when(up_goes(hop, part))
+            stream = jnp.where((chip == 0) & (hop > 0), 0, core)
+
+            @pl.when(down_goes(hop, part, stream))
             def _():
-                up_copy(hop, part).wait_send()
-
-            for stream in range(2):
-
-                @pl.when(down_goes(hop, part, stream))
-                def _():
-                    down_copy(hop, part, stream).wait_send()
-
-        for hop in range(1, 5):
-
-            @pl.when(up_comes(hop, part))
-            def _():
-                side_copy(chip - hop, part).wait_send()
-
-            for stream in range(2):
-
-                @pl.when(down_hands(hop, part, stream))
+                down_copy(hop, part, stream).wait_send()
+
+        @pl.when((chip == 0) & (core == 1))
+        def _():
+            for hop in range(1, 4):
+
+                @pl.when(down_goes(hop, part, 1))
+                def _():
+                    down_copy(hop, part, 1).wait_send()
+
+        @pl.when(chip >= 4)
+        def _():
+            for hop in range(2, 5):
+
+                @pl.when(down_hands(hop, part, core))
                 def _():
                     side_copy(lax.rem(chip + hop, CHIPS), part).wait_send()
 

time: 23.8 us -> 23.1 us (0.971)
  the two profiles are of different devices: /device:TPU:49 before, /device:TPU:57 now
where the time goes in v6:
time: 23.1 us; the launch traced here: 23 us
  Pallas kernels  22.2 us (96%)
  local copies, waits for them, and re-layouts  0.8 us (3%)
    pallas_call x1, Pallas kernels, per_device(): pl.pallas_call(kernel, out_shape=pltpu.VMEM((rows, width), jnp.bfloat16),...  22.2 us
    unnamed x1, local copies, waits for them, and re-layouts  0.8 us

profile of v6, /device:TPU:57, one launch (start us, length us, event | category | flops | bytes accessed | tf_op | source)
XLA Modules:
  0.0 23.0 jit_solution(15406098453887942633)
XLA Ops:
  0.0 22.2 %ring_attention.1 = bf16[256,1024]{1,0:T(8,128)(2,1)S(1)} custom-call(bf16[256,1024]{1,0:T(8,128)(2,1)} %q_ref.1, bf16[256,128]{1,0:T(8,128)(2,1)} %k_ref.1, bf16[256,128]{1,0:T(8,128)(2,1)} %v_ref.1, s32[2,128]{1,0:T(2,128)} %bitcast.1), custom_call_target="tpu_custom_call" | custom-call | flops 3489660928 | bytes 1048576 | tf_op jit(solution)/shard_map/ring_attention/pallas_call | solution.py:368
  22.2 0.8 %copy.6 = bf16[256,1024]{1,0:T(8,128)(2,1)} copy(bf16[256,1024]{1,0:T(8,128)(2,1)S(1)} %ring_attention.1) | data formatting | bytes 1048576

commit v7 on v6

--- a/solution.py
+++ b/solution.py
@@ -127,17 +127,17 @@
     q_in.start()
 
     def send_own(part):
+        @pl.when(chip <= 2)
+        def _():
+            down_copy(0, part, core).start()
+
         @pl.when(chip < CHIPS - 1)
         def _():
             up_copy(0, part).start()
 
-        @pl.when(chip <= LAST[part])
+        @pl.when((chip > 2) & (chip <= LAST[part]))
         def _():
             down_copy(0, part, core).start()
-
-        @pl.when(core == 0)
-        def _():
-            side_copy(chip, part).start()
 
     k_in.wait()
     pl.semaphore_wait(barrier, sum(partner.astype(jnp.int32) for partner in partners))
@@ -159,6 +159,11 @@
         at = rows + SEG + half * HD
         kv[me, at : at + HD, :] = turned[:, half * HD : (half + 1) * HD]
     send_own(1)
+
+    @pl.when(core == 0)
+    def _():
+        for part in range(2):
+            side_copy(chip, part).start()
 
     def inside(low, high):
         place = lax.broadcasted_iota(jnp.int32, (rows, HD), 0).astype(jnp.float32)

time: 23.1 us -> 23.1 us (level)
  no operation moved by 1% of the time
where the time goes in v7:
time: 23.1 us; the launch traced here: 23 us
  Pallas kernels  22.2 us (96%)
  local copies, waits for them, and re-layouts  0.8 us (3%)
    pallas_call x1, Pallas kernels, per_device(): pl.pallas_call(kernel, out_shape=pltpu.VMEM((rows, width), jnp.bfloat16),...  22.2 us
    unnamed x1, local copies, waits for them, and re-layouts  0.8 us

profile of v7, /device:TPU:57, one launch (start us, length us, event | category | flops | bytes accessed | tf_op | source)
XLA Modules:
  0.0 23.0 jit_solution(13481320631070464891)
XLA Ops:
  0.0 22.2 %ring_attention.1 = bf16[256,1024]{1,0:T(8,128)(2,1)S(1)} custom-call(bf16[256,1024]{1,0:T(8,128)(2,1)} %q_ref.1, bf16[256,128]{1,0:T(8,128)(2,1)} %k_ref.1, bf16[256,128]{1,0:T(8,128)(2,1)} %v_ref.1, s32[2,128]{1,0:T(2,128)} %bitcast.1), custom_call_target="tpu_custom_call" | custom-call | flops 3489660928 | bytes 1048576 | tf_op jit(solution)/shard_map/ring_attention/pallas_call | solution.py:373
  22.2 0.8 %copy.6 = bf16[256,1024]{1,0:T(8,128)(2,1)} copy(bf16[256,1024]{1,0:T(8,128)(2,1)S(1)} %ring_attention.1) | data formatting | bytes 1048576

commit v8 on v7

--- a/solution.py
+++ b/solution.py
@@ -279,8 +279,13 @@
 
                 relay_up(hop, part)
 
-                @pl.when(jnp.logical_not(first))
-                def _():
+                @pl.when((chip == 0) | (chip == 2))
+                def _():
+                    relay_down(hop, part)
+
+            @pl.when((chip >= 4) & (chip < CHIPS - 1))
+            def _():
+                for part in range(2):
                     relay_down(hop, part)
 
         pair = down_pair(hop)

time: 23.1 us -> 23.4 us (1.013); the launches traced: 23 us -> 23 us
  no operation moved by 1% of the time
where the time goes in v8:
time: 23.4 us; the launch traced here: 23 us
  Pallas kernels  22.2 us (95%)
  local copies, waits for them, and re-layouts  0.8 us (3%)
    pallas_call x1, Pallas kernels, per_device(): pl.pallas_call(kernel, out_shape=pltpu.VMEM((rows, width), jnp.bfloat16),...  22.2 us
    unnamed x1, local copies, waits for them, and re-layouts  0.8 us

profile of v8, /device:TPU:57, one launch (start us, length us, event | category | flops | bytes accessed | tf_op | source)
XLA Modules:
  0.0 23.0 jit_solution(5332707605972822056)
XLA Ops:
  0.0 22.2 %ring_attention.1 = bf16[256,1024]{1,0:T(8,128)(2,1)S(1)} custom-call(bf16[256,1024]{1,0:T(8,128)(2,1)} %q_ref.1, bf16[256,128]{1,0:T(8,128)(2,1)} %k_ref.1, bf16[256,128]{1,0:T(8,128)(2,1)} %v_ref.1, s32[2,128]{1,0:T(2,128)} %bitcast.1), custom_call_target="tpu_custom_call" | custom-call | flops 3489660928 | bytes 1048576 | tf_op jit(solution)/shard_map/ring_attention/pallas_call | solution.py:378
  22.2 0.8 %copy.6 = bf16[256,1024]{1,0:T(8,128)(2,1)} copy(bf16[256,1024]{1,0:T(8,128)(2,1)S(1)} %ring_attention.1) | data formatting | bytes 1048576

commit v9 on v7

--- a/solution.py
+++ b/solution.py
@@ -267,7 +267,7 @@
     def one_round(hop, carry):
         below_source = jnp.where(chip == 0, 0, chip - hop)
         above_source = lax.rem(chip + hop, CHIPS)
-        first = (chip == 1) | (chip == CHIPS - 1)
+        first = (chip == 1) | (chip == 5) | (chip == CHIPS - 1) | ((chip == CHIPS - 2) & (hop >= 3))
 
         @pl.when(hop >= 1)
         def _():

time: 23.1 us -> 23.1 us (level)
  no operation moved by 1% of the time
where the time goes in v9:
time: 23.1 us; the launch traced here: 23 us
  Pallas kernels  22.2 us (96%)
  local copies, waits for them, and re-layouts  0.8 us (3%)
    pallas_call x1, Pallas kernels, per_device(): pl.pallas_call(kernel, out_shape=pltpu.VMEM((rows, width), jnp.bfloat16),...  22.2 us
    unnamed x1, local copies, waits for them, and re-layouts  0.8 us

profile of v9, /device:TPU:57, one launch (start us, length us, event | category | flops | bytes accessed | tf_op | source)
XLA Modules:
  0.0 23.0 jit_solution(13761495844782372629)
XLA Ops:
  0.0 22.2 %ring_attention.1 = bf16[256,1024]{1,0:T(8,128)(2,1)S(1)} custom-call(bf16[256,1024]{1,0:T(8,128)(2,1)} %q_ref.1, bf16[256,128]{1,0:T(8,128)(2,1)} %k_ref.1, bf16[256,128]{1,0:T(8,128)(2,1)} %v_ref.1, s32[2,128]{1,0:T(2,128)} %bitcast.1), custom_call_target="tpu_custom_call" | custom-call | flops 3489660928 | bytes 1048576 | tf_op jit(solution)/shard_map/ring_attention/pallas_call | solution.py:373
  22.2 0.8 %copy.6 = bf16[256,1024]{1,0:T(8,128)(2,1)} copy(bf16[256,1024]{1,0:T(8,128)(2,1)S(1)} %ring_attention.1) | data formatting | bytes 1048576

commit v10 on v9

--- a/solution.py
+++ b/solution.py
@@ -287,7 +287,7 @@
         short = pair & (hop == 2) & (core == 1)
         doubles = jnp.where(short, 1, 2) * pair.astype(jnp.int32)
         alone = jnp.where(pair, 0, 2 * (chip >= hop).astype(jnp.int32))
-        alone = jnp.where(short, 1, jnp.where(hop == 0, core, alone))
+        alone = jnp.where(short, 1, jnp.where(hop == 0, 0, jnp.where(hop == 1, alone + core, alone)))
         alone = jnp.where(chip == 0, jnp.where(hop == 4, core, 0), alone)
         second = short | (hop == 0) | (chip == 0)
 
@@ -302,13 +302,14 @@
             return carry
 
         def one_block(i, carry):
-            other = (i == 1) | second
+            other = (i >= 1) | second
+            source = jnp.where((hop == 1) & (i == 2), chip, below_source)
 
             @pl.when(other)
             def _():
-                handed(below_source * 2 + 1 - core)
-
-            attend([below_source * 2 + jnp.where(other, 1 - core, core)])
+                handed(source * 2 + 1 - core)
+
+            attend([source * 2 + jnp.where(other, 1 - core, core)])
             return carry
 
         lax.fori_loop(0, doubles, one_double, 0)

time: 23.1 us -> 24.4 us (1.056)
  the two profiles are of different devices: /device:TPU:57 before, /device:TPU:429 now
where the time goes in v10:
time: 24.4 us; the launch traced here: 24.3 us
  Pallas kernels  23.5 us (96%)
  local copies, waits for them, and re-layouts  0.8 us (3%)
    pallas_call x1, Pallas kernels, per_device(): pl.pallas_call(kernel, out_shape=pltpu.VMEM((rows, width), jnp.bfloat16),...  23.5 us
    unnamed x1, local copies, waits for them, and re-layouts  0.8 us

profile of v10, /device:TPU:429, one launch (start us, length us, event | category | flops | bytes accessed | tf_op | source)
XLA Modules:
  0.0 24.3 jit_solution(11706219522495910928)
XLA Ops:
  0.0 23.5 %ring_attention.1 = bf16[256,1024]{1,0:T(8,128)(2,1)S(1)} custom-call(bf16[256,1024]{1,0:T(8,128)(2,1)} %q_ref.1, bf16[256,128]{1,0:T(8,128)(2,1)} %k_ref.1, bf16[256,128]{1,0:T(8,128)(2,1)} %v_ref.1, s32[2,128]{1,0:T(2,128)} %bitcast.1), custom_call_target="tpu_custom_call" | custom-call | flops 3489660928 | bytes 1048576 | tf_op jit(solution)/shard_map/ring_attention/pallas_call | solution.py:374
  23.5 0.8 %copy.6 = bf16[256,1024]{1,0:T(8,128)(2,1)} copy(bf16[256,1024]{1,0:T(8,128)(2,1)S(1)} %ring_attention.1) | data formatting | bytes 1048576
